TPU v7x, 128 devices: a whole 4x4x4 slice. The times are simulated.
128 devices in a mesh: rows: 32 (over z, x, core), cols: 4 (over y).
Axes of the slice: x: 4, y: 4, z: 4, core: 2. Of those that a mesh axis runs over, the one named last changes fastest.
Arguments:
- trial_block: bfloat16 [294912, 512], P('rows', 'cols'), may hold values from -6 to 6
- ham_blocks: bfloat16 [2304, 9, 128, 128], P('rows'), may hold values from -0.1875 to 0.1875
- partner: int32 [2304, 9], P('rows'), may hold values from 0 to 79, as said below
- live_slots: int32 [32], P('rows'), may hold values from 36 to 72, as said below
Outputs:
- filtered: bfloat16 [294912, 512], P('rows', 'cols')
- gram: float32 [512, 512], P('rows', 'cols')
Inputs may be any that keep to these rules, and one draw needn't show every extreme that they name: `partner`: each k of a slot s names a different slot of s + 4 - 4 to s + 8, and the first names s + 4 itself. `live_slots`: some owner has 72 live slots and another the least value.
All inputs are finite; a program needn't handle non-finite values.
Results may differ from a plain program's by a relative error of at most 0.007.
Values may be sent and summed in bfloat16 or wider, within the bound.
A program may use at most 128 MiB of HBM per device.

v0:
```python
import jax
import jax.numpy as jnp
from jax import lax
from jax.sharding import PartitionSpec as P

HW = 4


CENTER = 0.5
HALF_WIDTH = 1.5


def extended_2(cells, sides, width):
    for axis, dim in sides:
        count = lax.axis_size(axis)
        ends = count - 1
        head = lax.slice_in_dim(cells, 0, width, axis=dim)
        tail = lax.slice_in_dim(cells, cells.shape[dim] - width, cells.shape[dim], axis=dim)
        cells = jnp.concatenate(
            [
                lax.ppermute(tail, axis, [(i, (i + 1) % count) for i in range(ends)]),
                cells,
                lax.ppermute(head, axis, [((i + 1) % count, i) for i in range(ends)]),
            ],
            axis=dim,
        )
    return cells


def apply_operator(vectors, ham_blocks, partner):
    slot_count = ham_blocks.shape[0]
    rows_per = ham_blocks.shape[2]
    extended = extended_2(vectors, (("rows", 0),), HW * rows_per)
    windowed = extended.reshape(slot_count + 2 * HW, rows_per, vectors.shape[1])
    picked = windowed[partner]
    product = jnp.einsum("skab,skbc->sac", ham_blocks, picked, preferred_element_type=jnp.float32)
    return product.reshape(vectors.shape)


def body(trial_block, ham_blocks, partner, live_slots):
    slot_count = ham_blocks.shape[0]
    rows_per = ham_blocks.shape[2]
    live_count = live_slots[0]
    slot_ids = jnp.arange(slot_count, dtype=jnp.int32)
    keeps_slot = (slot_ids < HW) | (slot_ids >= HW + slot_count - live_count)
    row_keep = jnp.repeat(keeps_slot, rows_per)[:, None]
    start = jnp.where(row_keep, trial_block, jnp.zeros_like(trial_block))
    start_wide = start.astype(jnp.float32)
    first = jnp.where(
        row_keep,
        (apply_operator(start, ham_blocks, partner) - CENTER * start_wide) / HALF_WIDTH,
        0.0,
    ).astype(jnp.bfloat16)
    first_wide = first.astype(jnp.float32)
    second_wide = (
        2.0 * (apply_operator(first, ham_blocks, partner) - CENTER * first_wide) / HALF_WIDTH
        - start_wide
    )
    filtered = jnp.where(row_keep, second_wide, 0.0).astype(jnp.bfloat16)
    owner_count = lax.axis_size("rows")
    col_count = lax.axis_size("cols")
    total_rows = filtered.shape[0] * owner_count
    states = filtered.shape[1] * col_count
    shared = lax.all_to_all(filtered, "cols", split_axis=0, concat_axis=1, tiled=True)
    partial_gram = jnp.einsum("rs,rt->st", shared, shared, preferred_element_type=jnp.float32)
    arranged = partial_gram.reshape(
        owner_count, states // owner_count, col_count, states // col_count
    )
    arranged = arranged.transpose(0, 2, 1, 3).reshape(
        owner_count * col_count * (states // owner_count), states // col_count
    )
    tile = lax.psum_scatter(arranged, ("rows", "cols"), scatter_dimension=0, tiled=True)
    gram = tile / total_rows
    return (filtered, gram)


def solution(mesh):
    return jax.shard_map(
        body,
        mesh=mesh,
        in_specs=(P("rows", "cols"), P("rows", None, None, None), P("rows", None), P("rows")),
        out_specs=(P("rows", "cols"), P("rows", "cols")),
        check_vma=False,
    )
```

profile of v0, /device:TPU:1, one launch (start us, length us, event | category | flops | bytes accessed | tf_op | source)
XLA Modules:
  0.0 816.1 jit_solution(11656826593582830098)
XLA Ops:
  7.2 0.0 reduce-scatter.2.cloned.1.call-start
  7.9 0.1 broadcast_bitcast_fusion
  8.0 6.7 broadcast_select_fusion
  14.6 0.0 copy-start.3
  14.6 1.4 copy-done.3
  16.0 4.5 collective-permute-start
  20.6 1.9 collective-permute-start.1
  22.5 0.1 copy.7
  22.6 0.1 reshape.35
  22.8 4.1 collective-permute-done.1
  26.8 6.7 pad_maximum_fusion
  33.5 18.1 %gather_fusion = bf16[648,128,128]{2,1,0:T(8,128)(2,1)} fusion(bf16[80,128,128]{2,1,0:T(8,128)(2,1)S(1)} %bitcast.50, s32[1024]{0:T(1024)S(1)} %pad_clamp_fusion), kind=kCustom, calls=%fused_computation | custom fusion | bytes 42469920 | tf_op jit(solution)/shard_map/gather | solution.py:35
  51.7 0.0 copy-start.2
  51.7 18.4 %fusion.11 = f32[72,128,128,1]{1,2,3,0:T(8,128)} fusion(bf16[72,9,128,128]{3,2,1,0:T(8,128)(2,1)} %param.5, bf16[72,9,128,128]{3,2,1,0:T(8,128)(2,1)} %bitcast.53), kind=kOutput, calls=%fused_computation.24 | convolution fusion | flops 2717908992 | bytes 47185920 | tf_op jit(solution)/shard_map/skab,skbc->sac/dot_general | solution.py:36
  70.1 7.2 fusion.3
  77.3 0.0 copy-start
  77.3 1.9 collective-permute-start.2
  79.3 2.6 collective-permute-start.3
  81.9 3.7 collective-permute-done.3
  85.6 6.2 pad_maximum_fusion.1
  91.8 18.1 %gather_fusion.1 = bf16[648,128,128]{2,1,0:T(8,128)(2,1)} fusion(bf16[80,128,128]{2,1,0:T(8,128)(2,1)S(1)} %bitcast.51, s32[1024]{0:T(1024)S(1)} %pad_clamp_fusion), kind=kCustom, calls=%fused_computation.1 | custom fusion | bytes 42469920 | tf_op jit(solution)/shard_map/gather | solution.py:35
  109.9 0.0 copy-start.1
  109.9 18.5 %fusion.12 = f32[72,128,128,1]{1,2,3,0:T(8,128)} fusion(bf16[72,9,128,128]{3,2,1,0:T(8,128)(2,1)} %param.5, bf16[72,9,128,128]{3,2,1,0:T(8,128)(2,1)} %bitcast.52), kind=kOutput, calls=%fused_computation.25 | convolution fusion | flops 2717908992 | bytes 47185920 | tf_op jit(solution)/shard_map/skab,skbc->sac/dot_general | solution.py:36
  128.4 7.0 fusion.5
  135.4 0.0 copy-start.4
  135.4 1.4 copy-done.4
  136.8 31.6 %all_to_all.19 = bf16[4,2304,128]{2,1,0:T(8,128)(2,1)S(1)} all-to-all(bf16[4,2304,128]{2,1,0:T(8,128)(2,1)S(1)} %bitcast.55), channel_id=1, replica_groups=mesh['rows'=32,'cols'=4] {'cols'}, dimensions={0} | all-to-all | bytes 4718592 | tf_op jit(solution)/shard_map/all_to_all | solution.py:64
  168.4 2.5 copy.8
  170.9 4.8 fusion.7
  175.7 0.0 reduce-scatter.2.cloned.1.call-update
  175.7 632.2 %reduce-scatter.2.cloned.1.call-done = f32[16,128]{1,0:T(8,128)} async-done(((f32[2048,128]{1,0:T(8,128)}), f32[16,128]{1,0:T(8,128)}) %reduce-scatter.2.cloned.1.call-update) | async-done | bytes 8208 | tf_op jit(solution)/shard_map/reduce_scatter | solution.py:72
  807.9 1.3 broadcast_multiply_fusion
  (12 shorter events, 0.1 us)
Async XLA Ops:
  7.2 15.3 %copy-start.5 = (s32[72,9]{0,1:T(8,128)S(1)}, s32[72,9]{0,1:T(8,128)}, u32[]{:S(2)}) copy-start(s32[72,9]{0,1:T(8,128)} %param.6) | copy-start | bytes 7780
  7.2 800.8 %reduce-scatter.2.cloned.1.call-start = ((), (), s32[]{:S(2)}) async-start(), calls=%async_computation.2 | async-start | bytes 1056768 | tf_op jit(solution)/shard_map/reduce_scatter | solution.py:72
  14.6 1.4 copy-start.3
  16.0 6.7 collective-permute-start
  20.6 6.3 collective-permute-start.1
  51.7 18.5 %copy-start.2 = (bf16[9216,128]{1,0:T(8,128)(2,1)S(1)}, bf16[9216,128]{1,0:T(8,128)(2,1)}, u32[]{:S(2)}) copy-start(bf16[9216,128]{1,0:T(8,128)(2,1)} %param.4) | copy-start | bytes 7077892
  77.3 8.3 %copy-start = (bf16[9216,128]{1,0:T(8,128)(2,1)}, bf16[9216,128]{1,0:T(8,128)(2,1)S(1)}, u32[]{:S(2)}) copy-start(bf16[9216,128]{1,0:T(8,128)(2,1)S(1)} %fusion.3) | copy-start | bytes 7077892
  77.3 4.5 collective-permute-start.2
  79.3 6.3 collective-permute-start.3
  109.9 18.5 %copy-start.1 = (bf16[9216,128]{1,0:T(8,128)(2,1)S(1)}, bf16[9216,128]{1,0:T(8,128)(2,1)}, u32[]{:S(2)}) copy-start(bf16[9216,128]{1,0:T(8,128)(2,1)} %copy-done) | copy-start | bytes 7077892
  135.4 1.4 copy-start.4
Sparse Core Ops, SparseCore 0:
  175.8 632.0 reduce-scatter.1
where the time goes:
time: 824 us; the launch traced here: 816 us
  waiting for transfers between devices  640 us (78%)
  local copies, waits for them, and re-layouts  41.9 us (5%)
  matrix products  41.7 us (5%)
  other arithmetic  35 us (4%)
  blocking collectives  31.6 us (4%)
  between operations  14.9 us (2%)
  starting transfers between devices  11 us (1%)
    reduce_scatter x1, waiting for transfers between devices, body(): lax.psum_scatter(arranged, ('rows', 'cols'), scatter_dimension=0, tiled=T...  632 us
    dot_general x2, matrix products, apply_operator(): jnp.einsum('skab,skbc->sac', ham_blocks, picked, preferred_element_type=j...  36.9 us
    gather x2, local copies, waits for them, and re-layouts, apply_operator(): picked = windowed[partner]  36.2 us
    all_to_all x1, blocking collectives, body(): lax.all_to_all(filtered, 'cols', split_axis=0, concat_axis=1, tiled=True)  31.6 us
  transfers between devices with their start and end apart: 5, of which 3 were waited for; matrix products, arithmetic and copies ran while one was open for 0% of the time, Pallas kernels for 0%

commit v1 on v0

v1 whole, which is shorter than its diff:
```python
import functools

import jax
import jax.numpy as jnp
from jax import lax
from jax.experimental import pallas as pl
from jax.experimental.pallas import tpu as pltpu
from jax.sharding import PartitionSpec as P

MESH = pl.DeviceIdType.MESH
HW = 4
B = 128
S = 72
K = 9
GS = 4
NG = S // GS
NS = 512
CENTER = 0.5
HALF_WIDTH = 1.5
BF = jnp.bfloat16
F32 = jnp.float32


def kernel(trial, ham, partner, live, filt, gram,
           hbuf, v0, v1, land0, land1, fout, recv, gacc,
           core_out, core_in, acc, a_out, a_in, b_out, b_in,
           a2, b2, a2_out, b2_out, a3_in, b3_in, tile, tile_in,
           h_sem, t_sem, f_sem, halo_s, halo_r, y_s, y_r, c_s, c_r, p_s, p_r, q_s, q_r, w_s, w_r):
    row = lax.axis_index("rows")
    col = lax.axis_index("cols")
    core = lax.rem(row, 2)
    px = lax.rem(row // 2, 4)
    pz = row // 8
    after = (lax.rem(row + 1, 32), col)
    before = (lax.rem(row + 31, 32), col)
    mate = (row + 1 - 2 * core, col)

    def at_y(d):
        return (row, lax.rem(col + d, 4))

    def at_x(d):
        return (pz * 8 + lax.rem(px + d, 4) * 2 + core, col)

    def at_z(d):
        return (lax.rem(pz + d, 4) * 8 + px * 2 + core, col)

    peers = [after, before, mate] + [f(d) for f in (at_x, at_y, at_z) for d in (1, 2, 3)]
    barrier = pltpu.get_barrier_semaphore()
    for peer in peers:
        pl.semaphore_signal(barrier, inc=1, device_id=peer, device_id_type=MESH)

    def remote(src, dst, ssem, rsem, peer):
        return pltpu.make_async_remote_copy(
            src_ref=src, dst_ref=dst, send_sem=ssem, recv_sem=rsem,
            device_id=peer, device_id_type=MESH)

    load_trial = pltpu.make_async_copy(trial, v0.at[pl.ds(HW, S)], t_sem.at[0])
    load_trial.start()

    def load_ham(b):
        part = pl.ds(b * GS, GS)
        return pltpu.make_async_copy(ham.at[part], hbuf.at[part], h_sem.at[b])

    def block_of(i):
        return lax.rem(i + 1, NG)

    lax.fori_loop(0, NG, lambda i, c: (load_ham(block_of(i)).start(), c)[1], 0)
    load_trial.wait()

    count = live[0]

    def keep(s):
        return (s < HW) | (s >= HW + S - count)

    def mask(s, c):
        v0[s + HW] = jnp.where(keep(s), v0[s + HW].astype(F32), 0.0).astype(BF)
        return c

    lax.fori_loop(HW, S - 32, mask, 0)

    def product(src, s):
        lhs = jnp.concatenate([hbuf[s, k] for k in range(K)], axis=1)
        rhs = jnp.concatenate([src[partner[s, k]] for k in range(K)], axis=0)
        return jnp.dot(lhs, rhs, preferred_element_type=F32)

    def first_step(b):
        for j in range(GS):
            s = b * GS + j
            value = (product(v0, s) - CENTER * v0[s + HW].astype(F32)) * (1.0 / HALF_WIDTH)
            v1[s + HW] = jnp.where(keep(s), value, 0.0).astype(BF)

    def second_step(g):
        for j in range(GS):
            s = g * GS + j
            value = (product(v1, s) - CENTER * v1[s + HW].astype(F32)) * (2.0 / HALF_WIDTH)
            value = value - v0[s + HW].astype(F32)
            fout[s] = jnp.where(keep(s), value, 0.0).astype(BF)

    def store_out(g):
        part = pl.ds(g * GS, GS)
        return pltpu.make_async_copy(fout.at[part], filt.at[part], f_sem.at[g])

    def to_col(g, t, d):
        there = lax.rem(col + d, 4)
        return remote(fout.at[g * GS + there], recv.at[t, col], y_s.at[t, d - 1], y_r.at[t, d - 1], at_y(d))

    def from_col(t, d):
        origin = lax.rem(col + 4 - d, 4)
        return remote(fout.at[0], recv.at[t, origin], y_s.at[t, d - 1], y_r.at[t, d - 1], at_y(d))

    def hand_out(g, t):
        for d in (2, 1, 3):
            to_col(g, t, d).start()
        store_out(g).start()
        recv[t, col] = fout[g * GS + col]

    def prologue(i, c):
        b = block_of(i)
        load_ham(b).wait()
        first_step(b)
        return c

    lax.fori_loop(0, 2, prologue, 0)

    pl.semaphore_wait(barrier, len(peers))

    def halo(src, first, land, n):
        return (
            remote(src.at[pl.ds(first + S - HW, HW)], land.at[0], halo_s.at[n], halo_r.at[n], after),
            remote(src.at[pl.ds(first, HW)], land.at[1], halo_s.at[n + 1], halo_r.at[n + 1], before),
        )

    def place(land, dst):
        for j in range(HW):
            dst[j] = jnp.where(row > 0, land[0, j].astype(F32), 0.0).astype(BF)
            dst[j + HW + S] = jnp.where(row < 31, land[1, j].astype(F32), 0.0).astype(BF)

    halo0 = halo(trial, 0, land0, 0)
    for copy in halo0:
        copy.start()

    def main(i, c):
        b = block_of(i)

        @pl.when(i == NG - 2)
        def _():
            for copy in halo0:
                copy.wait()
            place(land0, v0)

        load_ham(b).wait()
        first_step(b)
        g = jnp.where(i == NG - 1, 1, i)
        second_step(g)
        hand_out(g, i - 2)
        return c

    lax.fori_loop(2, NG, main, 0)

    halo1 = halo(v1, HW, land1, 2)
    for copy in halo1:
        copy.start()
    for copy in halo1:
        copy.wait()
    place(land1, v1)

    def ends(n, c):
        g = n * (NG - 1)
        second_step(g)
        hand_out(g, NG - 2 + n)
        return c

    lax.fori_loop(0, 2, ends, 0)

    gacc[...] = jnp.zeros_like(gacc)

    def gram_step(n, c):
        for u in range(2):
            for d in (1, 2, 3):
                from_col(2 * n + u, d).wait_recv()
        rows = [jnp.concatenate([recv[2 * n + u, q] for q in range(4)], axis=1) for u in range(2)]
        x = jnp.concatenate(rows, axis=0)
        part = lax.dot_general(x, x, (((0,), (0,)), ((), ())), preferred_element_type=F32)
        gacc[...] += part.reshape(gacc.shape)
        return c

    lax.fori_loop(0, NG // 2, gram_step, 0)

    for n in range(16):
        core_out[n] = gacc[2 * n + 1 - core].astype(BF)
    to_mate = remote(core_out, core_in, c_s.at[0], c_r.at[0], mate)
    to_mate.start()
    to_mate.wait()

    for n in range(16):
        acc[n] = gacc[2 * n + core] + core_in[n].astype(F32)
    copies = []
    for d in (2, 1, 3):
        there = lax.rem(px + d, 4)
        for z in range(4):
            a_out[d - 1, z] = acc[z * 4 + there, :, 0:256].astype(BF)
        copies.append(remote(a_out.at[d - 1], a_in.at[d - 1], p_s.at[0, d - 1], p_r.at[0, d - 1], at_x(d)))
        copies[-1].start()
        there = lax.rem(pz + d, 4)
        for x in range(4):
            b_out[d - 1, x] = acc[there * 4 + x, :, 256:512].astype(BF)
        copies.append(remote(b_out.at[d - 1], b_in.at[d - 1], p_s.at[1, d - 1], p_r.at[1, d - 1], at_z(d)))
        copies[-1].start()
    for copy in copies:
        copy.wait()
    for n in range(4):
        a2[n] = acc[n * 4 + px, :, 0:256] + sum(a_in[d, n].astype(F32) for d in range(3))
        b2[n] = acc[pz * 4 + n, :, 256:512] + sum(b_in[d, n].astype(F32) for d in range(3))
    copies = []
    for d in (2, 1, 3):
        a2_out[d - 1] = a2[lax.rem(pz + d, 4)].astype(BF)
        copies.append(remote(a2_out.at[d - 1], a3_in.at[d - 1], q_s.at[0, d - 1], q_r.at[0, d - 1], at_z(d)))
        copies[-1].start()
        b2_out[d - 1] = b2[lax.rem(px + d, 4)].astype(BF)
        copies.append(remote(b2_out.at[d - 1], b3_in.at[d - 1], q_s.at[1, d - 1], q_r.at[1, d - 1], at_x(d)))
        copies[-1].start()
    for copy in copies:
        copy.wait()
    a3 = a2[pz] + sum(a3_in[d].astype(F32) for d in range(3))
    b3 = b2[px] + sum(b3_in[d].astype(F32) for d in range(3))
    for q in range(2):
        tile[q] = a3[:, q * 128:(q + 1) * 128]
        tile[q + 2] = b3[:, q * 128:(q + 1) * 128]

    copies = [
        remote(tile.at[lax.rem(col + d, 4)], tile_in.at[d - 1], w_s.at[d - 1], w_r.at[d - 1], at_y(d))
        for d in (2, 1, 3)
    ]
    for copy in copies:
        copy.start()
    for copy in copies:
        copy.wait()
    gram[...] = (tile[col] + (tile_in[0] + tile_in[1] + tile_in[2])) * (1.0 / (32 * S * B))

    def finish(t, c):
        for d in (1, 2, 3):
            from_col(t, d).wait_send()
        store_out(t).wait()
        return c

    lax.fori_loop(0, NG, finish, 0)


def body(trial_block, ham_blocks, partner, live_slots):
    dma = pltpu.SemaphoreType.DMA
    any_space = pl.BlockSpec(memory_space=pl.ANY)
    smem = pl.BlockSpec(memory_space=pltpu.SMEM)
    filtered, gram = pl.pallas_call(
        kernel,
        out_shape=(
            jax.ShapeDtypeStruct((S, B, B), BF),
            jax.ShapeDtypeStruct((16, 128), F32),
        ),
        in_specs=[any_space, any_space, smem, smem],
        out_specs=(any_space, pl.BlockSpec(memory_space=pltpu.VMEM)),
        scratch_shapes=[
            pltpu.VMEM((S, K, B, B), BF),
            pltpu.VMEM((S + 2 * HW, B, B), BF),
            pltpu.VMEM((S + 2 * HW, B, B), BF),
            pltpu.VMEM((2, HW, B, B), BF),
            pltpu.VMEM((2, HW, B, B), BF),
            pltpu.VMEM((S, B, B), BF),
            pltpu.VMEM((NG, 4, B, B), BF),
            pltpu.VMEM((32, 16, NS), F32),
            pltpu.VMEM((16, 16, NS), BF),
            pltpu.VMEM((16, 16, NS), BF),
            pltpu.VMEM((16, 16, NS), F32),
            pltpu.VMEM((3, 4, 16, 256), BF),
            pltpu.VMEM((3, 4, 16, 256), BF),
            pltpu.VMEM((3, 4, 16, 256), BF),
            pltpu.VMEM((3, 4, 16, 256), BF),
            pltpu.VMEM((4, 16, 256), F32),
            pltpu.VMEM((4, 16, 256), F32),
            pltpu.VMEM((3, 16, 256), BF),
            pltpu.VMEM((3, 16, 256), BF),
            pltpu.VMEM((3, 16, 256), BF),
            pltpu.VMEM((3, 16, 256), BF),
            pltpu.VMEM((4, 16, 128), F32),
            pltpu.VMEM((3, 16, 128), F32),
            dma((NG,)),
            dma((1,)),
            dma((NG,)),
            dma((4,)),
            dma((4,)),
            dma((NG, 3)),
            dma((NG, 3)),
            dma((1,)),
            dma((1,)),
            dma((2, 3)),
            dma((2, 3)),
            dma((2, 3)),
            dma((2, 3)),
            dma((3,)),
            dma((3,)),
        ],
        compiler_params=pltpu.CompilerParams(
            collective_id=0, has_side_effects=True, vmem_limit_bytes=50 << 20),
        name="filter_gram",
    )(trial_block.reshape(S, B, B), ham_blocks, partner, live_slots)
    return filtered.reshape(S * B, B), gram


def solution(mesh):
    return jax.shard_map(
        body,
        mesh=mesh,
        in_specs=(P("rows", "cols"), P("rows", None, None, None), P("rows", None), P("rows")),
        out_specs=(P("rows", "cols"), P("rows", "cols")),
        check_vma=False,
    )
```

time: 824 us -> 56.6 us (0.07)
  waiting for transfers between devices: 640 us -> 0 us
  Pallas kernels: 0 us -> 51.6 us
  matrix products: 41.7 us -> 0 us
  local copies, waits for them, and re-layouts: 41.9 us -> 2.79 us
  other arithmetic: 35 us -> 0 us
  blocking collectives: 31.6 us -> 0 us
  between operations: 14.9 us -> 1.29 us
  starting transfers between devices: 11 us -> 0 us
    reduce_scatter x1 -> x0, waiting for transfers between devices: 632 us -> none  [body(): lax.psum_scatter(arranged, ('rows', 'cols'), scatter_dimension=0, tiled=T...]
    pallas_call x0 -> x1, Pallas kernels: none -> 51.6 us  [body(): pl.pallas_call(kernel, out_shape=(jax.ShapeDtypeStruct((S, B, B), BF), ja...]
    dot_general x3 -> x0, matrix products: 41.7 us -> none  [the longest x2 36.9 us: apply_operator(): jnp.einsum('skab,skbc->sac', ham_blocks, picked, preferred_element_type=j...]
    gather x2 -> x0, local copies, waits for them, and re-layouts: 36.2 us -> none  [apply_operator(): picked = windowed[partner]]
    all_to_all x1 -> x0, blocking collectives: 31.6 us -> none  [body(): lax.all_to_all(filtered, 'cols', split_axis=0, concat_axis=1, tiled=True)]
    convert_element_type x2 -> x0, other arithmetic: 14.2 us -> none  [the longest x1 7.16 us: body(): first = jnp.where(row_keep, (apply_operator(start, ham_blocks, partner) -...]
    concatenate x2 -> x0, other arithmetic: 12.9 us -> none  [extended_2(): jnp.concatenate([lax.ppermute(tail, axis, [(i, (i + 1) % count) for i in...]
    ppermute x4 -> x0, starting transfers between devices: 10.9 us -> none  [the longest x2 6.43 us: extended_2(): lax.ppermute(tail, axis, [(i, (i + 1) % count) for i in range(ends)])]
  transfers between devices with their start and end apart: 5 -> 0, of which waited for: 3 -> 0; matrix products, arithmetic and copies ran while one was open for 0% -> 0% of each run, Pallas kernels for 0% -> 0%
where the time goes in v1:
time: 56.6 us; the launch traced here: 55.7 us
  Pallas kernels  51.6 us (91%)
  local copies, waits for them, and re-layouts  2.79 us (5%)
  between operations  1.29 us (2%)
    pallas_call x1, Pallas kernels, body(): pl.pallas_call(kernel, out_shape=(jax.ShapeDtypeStruct((S, B, B), BF), ja...  51.6 us
    unnamed x3, local copies, waits for them, and re-layouts  2.79 us

profile of v1, /device:TPU:1, one launch (start us, length us, event | category | flops | bytes accessed | tf_op | source)
XLA Modules:
  0.0 55.7 jit_solution(5376314980156836930)
XLA Ops:
  1.3 0.8 %copy.6.partner = s32[72,9]{1,0:T(8,128)S(1)} copy(s32[72,9]{0,1:T(8,128)} %param.6) | data formatting | bytes 5184 | tf_op args[2]
  2.1 51.6 %filter_gram.1 = (bf16[72,128,128]{2,1,0:T(8,128)(2,1)S(1)}, f32[16,128]{1,0:T(8,128)S(1)}) custom-call(bf16[72,128,128]{2,1,0:T(8,128)(2,1)} %bitcast.3, bf16[72,9,128,128]{3,2,1,0:T(8,128)(2,1)} %ham.1, s32[72,9]{1,0:T(8,128)S(1)} %copy.6.partner, s32[1]{0:T(128)S(6)} %copy.9.live), custom_call_target="tpu_custom_call" | custom-call | tf_op jit(solution)/shard_map/filter_gram/pallas_call | solution.py:253
  53.7 1.4 %copy.10 = bf16[9216,128]{1,0:T(8,128)(2,1)} copy(bf16[9216,128]{1,0:T(8,128)(2,1)S(1)} %bitcast.2) | data formatting | bytes 4718592
  55.1 0.6 %copy.11 = f32[16,128]{1,0:T(8,128)} copy(f32[16,128]{1,0:T(8,128)S(1)} %get-tuple-element.9) | data formatting | bytes 16384

commit v2 on v1

v2 whole, which is shorter than its diff:
```python
import functools

import jax
import jax.numpy as jnp
from jax import lax
from jax.experimental import pallas as pl
from jax.experimental.pallas import tpu as pltpu
from jax.sharding import PartitionSpec as P

MESH = pl.DeviceIdType.MESH
HW = 4
B = 128
S = 72
K = 9
GS = 4
NG = S // GS
HEAD = 20
NS = 512
CENTER = 0.5
HALF_WIDTH = 1.5
BF = jnp.bfloat16
F32 = jnp.float32


def kernel(trial, ham, partner_in, live_in, filt, gram,
           partner, live, hbuf, v0a, v0, v1, land0, land1, recv, gacc,
           core_out, core_in, tiles_out, tiles_in, own,
           m_sem, h_sem, t_sem, halo_s, halo_r, y_s, y_r, c_s, c_r, p_s, p_r):
    row = lax.axis_index("rows")
    col = lax.axis_index("cols")
    core = lax.rem(row, 2)
    px = lax.rem(row // 2, 4)
    pz = row // 8
    after = (lax.rem(row + 1, 32), col)
    before = (lax.rem(row + 31, 32), col)
    mate = (row + 1 - 2 * core, col)

    def at_y(d):
        return (row, lax.rem(col + d, 4))

    def at_plane(dz, dx):
        return (lax.rem(pz + dz, 4) * 8 + lax.rem(px + dx, 4) * 2 + core, col)

    peers = [after, before, mate] + [at_y(d) for d in (1, 2, 3)]
    peers += [at_plane(n // 4, n % 4) for n in range(1, 16)]
    barrier = pltpu.get_barrier_semaphore()
    for peer in peers:
        pl.semaphore_signal(barrier, inc=1, device_id=peer, device_id_type=MESH)

    def remote(src, dst, ssem, rsem, peer):
        return pltpu.make_async_remote_copy(
            src_ref=src, dst_ref=dst, send_sem=ssem, recv_sem=rsem,
            device_id=peer, device_id_type=MESH)

    def load_ham(b):
        part = pl.ds(b * GS, GS)
        return pltpu.make_async_copy(ham.at[part], hbuf.at[part], h_sem.at[b])

    def block_of(i):
        return jnp.where(i < 7, i + 1, jnp.where(i < 9, (8 - i) * (NG - 1), i - 1))

    def start_ham(i, c):
        load_ham(block_of(i)).start()
        return c

    load_partner = pltpu.make_async_copy(partner_in, partner, m_sem.at[0])
    live = live_in
    load_head = pltpu.make_async_copy(trial.at[pl.ds(0, HEAD)], v0a.at[pl.ds(HW, HEAD)], t_sem.at[0])
    load_trial = pltpu.make_async_copy(trial, v0.at[pl.ds(HW, S)], t_sem.at[1])
    load_partner.start()
    load_head.start()
    for i in range(3):
        load_ham(block_of(i)).start()
    load_trial.start()
    lax.fori_loop(3, NG, start_ham, 0)
    count = live[0]

    def keep(s):
        return (s < HW) | (s >= HW + S - count)

    def mask(ref, s):
        ref[s + HW] = jnp.where(keep(s), ref[s + HW].astype(F32), 0.0).astype(BF)

    def product(src, s):
        lhs = jnp.concatenate([hbuf[s, k] for k in range(K)], axis=1)
        rhs = jnp.concatenate([src[partner[k, s]] for k in range(K)], axis=0)
        return jnp.dot(lhs, rhs, preferred_element_type=F32)

    def first_step(b, src):
        for j in range(GS):
            s = b * GS + j
            value = (product(src, s) - CENTER * src[s + HW].astype(F32)) * (1.0 / HALF_WIDTH)
            v1[s + HW] = jnp.where(keep(s), value, 0.0).astype(BF)

    def second_step(g):
        for j in range(GS):
            s = g * GS + j
            value = (product(v1, s) - CENTER * v1[s + HW].astype(F32)) * (2.0 / HALF_WIDTH)
            value = value - v0[s + HW].astype(F32)
            filt[s] = jnp.where(keep(s), value, 0.0).astype(BF)

    def to_col(g, t, d):
        there = lax.rem(col + d, 4)
        return remote(filt.at[g * GS + there], recv.at[t, col], y_s.at[t, d - 1], y_r.at[t, d - 1], at_y(d))

    def from_col(t, d):
        origin = lax.rem(col + 4 - d, 4)
        return remote(filt.at[0], recv.at[t, origin], y_s.at[t, d - 1], y_r.at[t, d - 1], at_y(d))

    def hand_out(g, t):
        for d in (2, 1, 3):
            to_col(g, t, d).start()
        recv[t, col] = filt[g * GS + col]

    load_head.wait()
    lax.fori_loop(HW, HEAD, lambda s, c: (mask(v0a, s), c)[1], 0)
    load_partner.wait()

    def prologue(i, c):
        b = block_of(i)
        load_ham(b).wait()
        first_step(b, v0a)
        return c

    lax.fori_loop(0, 3, prologue, 0)
    load_trial.wait()
    lax.fori_loop(HW, S - 32, lambda s, c: (mask(v0, s), c)[1], 0)
    second_step(2)
    pl.semaphore_wait(barrier, len(peers))
    hand_out(2, 0)

    def halo(src, first, land, n):
        return (
            remote(src.at[pl.ds(first + S - HW, HW)], land.at[0], halo_s.at[n], halo_r.at[n], after),
            remote(src.at[pl.ds(first, HW)], land.at[1], halo_s.at[n + 1], halo_r.at[n + 1], before),
        )

    def place(land, dst):
        for j in range(HW):
            dst[j] = jnp.where(row > 0, land[0, j].astype(F32), 0.0).astype(BF)
            dst[j + HW + S] = jnp.where(row < 31, land[1, j].astype(F32), 0.0).astype(BF)

    halo0 = halo(trial, 0, land0, 0)
    for copy in halo0:
        copy.start()

    def main(i, c):
        b = i + 1
        load_ham(b).wait()
        first_step(b, v0)
        second_step(i)
        hand_out(i, i - 2)
        return c

    lax.fori_loop(3, 7, main, 0)

    for copy in halo0:
        copy.wait()
    place(land0, v0)

    def outer(n, c):
        b = (1 - n) * (NG - 1)
        load_ham(b).wait()
        first_step(b, v0)
        return c

    lax.fori_loop(0, 2, outer, 0)
    halo1 = halo(v1, HW, land1, 2)
    for copy in halo1:
        copy.start()

    lax.fori_loop(7, NG - 2, main, 0)

    def last(n, c):
        g = jnp.where(n == 0, NG - 2, jnp.where(n < 3, 2 - n, NG - 1))

        @pl.when(n == 2)
        def _():
            for copy in halo1:
                copy.wait()
            place(land1, v1)

        second_step(g)
        hand_out(g, NG - 4 + n)
        return c

    lax.fori_loop(0, 4, last, 0)

    gacc[...] = jnp.zeros_like(gacc)

    def gram_step(first, groups):
        for u in range(groups):
            for d in (1, 2, 3):
                from_col(first + u, d).wait_recv()
        rows = [jnp.concatenate([recv[first + u, q] for q in range(4)], axis=1) for u in range(groups)]
        x = jnp.concatenate(rows, axis=0)
        part = lax.dot_general(x, x, (((0,), (0,)), ((), ())), preferred_element_type=F32)
        gacc[...] += part.reshape(gacc.shape)

    lax.fori_loop(0, NG // 2, lambda n, c: (gram_step(2 * n, 2), c)[1], 0)

    def to_mate(z):
        part = pl.ds(z * 4, 4)
        return remote(core_out.at[part], core_in.at[part], c_s.at[z], c_r.at[z], mate)

    for z in range(4):
        for n in range(4 * z, 4 * z + 4):
            core_out[n] = gacc[2 * n + 1 - core].astype(BF)
        to_mate(z).start()

    me = pz * 4 + px
    tiles_in[me * 4 + col] = jnp.zeros((16, 128), BF)

    def send_tile(n, q):
        peer = ((n // 4) * 8 + lax.rem(n, 4) * 2 + core, q)
        return remote(tiles_out.at[n * 4 + q], tiles_in.at[me * 4 + col], p_s.at[0], p_r.at[0], peer)

    for z in range(4):
        to_mate(z).wait_recv()
        for n in range(4 * z, 4 * z + 4):
            total = gacc[2 * n + core] + core_in[n].astype(F32)
            for q in range(4):
                tiles_out[n * 4 + q] = total[:, q * 128:(q + 1) * 128].astype(BF)

        def send(m, c):
            n = z * 4 + m // 4
            q = lax.rem(m, 4)

            @pl.when((n != me) | (q != col))
            def _():
                send_tile(n, q).start()

            return c

        lax.fori_loop(0, 16, send, 0)
    total = gacc[2 * me + core] + core_in[me].astype(F32)
    for q in range(4):
        own[q] = total[:, q * 128:(q + 1) * 128]

    def finish(t, c):
        for d in (1, 2, 3):
            from_col(t, d).wait_send()
        return c

    lax.fori_loop(0, NG, finish, 0)
    for z in range(4):
        to_mate(z).wait_send()
    rest = remote(tiles_out.at[pl.ds(0, 63)], tiles_in.at[pl.ds(0, 63)], p_s.at[0], p_r.at[0], mate)
    rest.wait_recv()
    total = own[col]
    for n in range(64):
        total = total + tiles_in[n].astype(F32)
    gram[...] = total * (1.0 / (32 * S * B))
    rest.wait_send()


def store(filt, gram, filt_out, gram_out, sem):
    copies = [
        pltpu.make_async_copy(filt.at[pl.ds(n * (S // 4), S // 4)], filt_out.at[pl.ds(n * (S // 4), S // 4)], sem.at[n])
        for n in range(4)
    ]
    copies.append(pltpu.make_async_copy(gram, gram_out, sem.at[4]))
    for copy in copies:
        copy.start()
    for copy in copies:
        copy.wait()


def body(trial_block, ham_blocks, partner, live_slots):
    dma = pltpu.SemaphoreType.DMA
    hbm = pl.BlockSpec(memory_space=pltpu.HBM)
    vmem = pl.BlockSpec(memory_space=pltpu.VMEM)
    shapes = (jax.ShapeDtypeStruct((S, B, B), BF), jax.ShapeDtypeStruct((16, 128), F32))
    filtered, gram = pl.pallas_call(
        kernel,
        out_shape=shapes,
        in_specs=[hbm, hbm, hbm, pl.BlockSpec(memory_space=pltpu.SMEM)],
        out_specs=(vmem, vmem),
        scratch_shapes=[
            pltpu.SMEM((K, S), jnp.int32),
            pltpu.SMEM((1,), jnp.int32),
            pltpu.VMEM((S, K, B, B), BF),
            pltpu.VMEM((HEAD + HW, B, B), BF),
            pltpu.VMEM((S + 2 * HW, B, B), BF),
            pltpu.VMEM((S + 2 * HW, B, B), BF),
            pltpu.VMEM((2, HW, B, B), BF),
            pltpu.VMEM((2, HW, B, B), BF),
            pltpu.VMEM((NG, 4, B, B), BF),
            pltpu.VMEM((32, 16, NS), F32),
            pltpu.VMEM((16, 16, NS), BF),
            pltpu.VMEM((16, 16, NS), BF),
            pltpu.VMEM((64, 16, 128), BF),
            pltpu.VMEM((64, 16, 128), BF),
            pltpu.VMEM((4, 16, 128), F32),
            dma((2,)),
            dma((NG,)),
            dma((2,)),
            dma((4,)),
            dma((4,)),
            dma((NG, 3)),
            dma((NG, 3)),
            dma((4,)),
            dma((4,)),
            dma((1,)),
            dma((1,)),
        ],
        compiler_params=pltpu.CompilerParams(
            collective_id=0, has_side_effects=True, vmem_limit_bytes=48 << 20),
        name="filter_gram",
    )(*[pltpu.with_memory_space_constraint(a, pltpu.HBM) for a in (trial_block.reshape(S, B, B), ham_blocks, partner.T)], live_slots)
    filtered, gram = pl.pallas_call(
        store,
        out_shape=shapes,
        in_specs=[vmem, vmem],
        out_specs=(hbm, hbm),
        scratch_shapes=[dma((5,))],
        name="store",
    )(*[pltpu.with_memory_space_constraint(a, pltpu.VMEM) for a in (filtered, gram)])
    return filtered.reshape(S * B, B), gram


def solution(mesh):
    return jax.shard_map(
        body,
        mesh=mesh,
        in_specs=(P("rows", "cols"), P("rows", None, None, None), P("rows", None), P("rows")),
        out_specs=(P("rows", "cols"), P("rows", "cols")),
        check_vma=False,
    )
```

time: 56.6 us -> 50 us (0.88); the launches traced: 55.7 us -> 49.9 us
  Pallas kernels: 51.6 us -> 48.6 us
  local copies, waits for them, and re-layouts: 2.79 us -> 0 us
    pallas_call x1 -> x2, Pallas kernels: 51.6 us -> 48.6 us  [the longest x1 47.2 us: body(): pl.pallas_call(kernel, out_shape=shapes, in_specs=[hbm, hbm, hbm, pl.Bloc...]
    unnamed x3 -> x0, local copies, waits for them, and re-layouts: 2.79 us -> none
where the time goes in v2:
time: 50 us; the launch traced here: 49.9 us
  Pallas kernels  48.6 us (97%)
  between operations  1.28 us (3%)
    pallas_call x1, Pallas kernels, body(): pl.pallas_call(kernel, out_shape=shapes, in_specs=[hbm, hbm, hbm, pl.Bloc...  47.2 us
    pallas_call x1, Pallas kernels, body(): pl.pallas_call(store, out_shape=shapes, in_specs=[vmem, vmem], out_specs=...  1.45 us

profile of v2, /device:TPU:1, one launch (start us, length us, event | category | flops | bytes accessed | tf_op | source)
XLA Modules:
  0.0 49.9 jit_solution(13770932047971067971)
XLA Ops:
  1.3 47.2 %filter_gram.1 = (bf16[72,128,128]{2,1,0:T(8,128)(2,1)S(1)}, f32[16,128]{1,0:T(8,128)S(1)}) custom-call(bf16[72,128,128]{2,1,0:T(8,128)(2,1)} %bitcast.3, bf16[72,9,128,128]{3,2,1,0:T(8,128)(2,1)} %ham.1, s32[9,72]{1,0:T(8,128)} %bitcast.4, s32[1]{0:T(128)S(6)} %copy.6.live_in), custom_call_target="tpu_custom_call" | custom-call | tf_op jit(solution)/shard_map/filter_gram/pallas_call | solution.py:274
  48.5 1.4 %store.1 = (bf16[72,128,128]{2,1,0:T(8,128)(2,1)}, f32[16,128]{1,0:T(8,128)}) custom-call(bf16[72,128,128]{2,1,0:T(8,128)(2,1)S(1)} %get-tuple-element.6.filt, f32[16,128]{1,0:T(8,128)S(1)} %get-tuple-element.7.gram), custom_call_target="tpu_custom_call" | custom-call | tf_op jit(solution)/shard_map/store/pallas_call | solution.py:311

commit v3 on v2

--- a/solution.py
+++ b/solution.py
@@ -14,6 +14,7 @@
 K = 9
 GS = 4
 NG = S // GS
+MID = 9
 HEAD = 20
 NS = 512
 CENTER = 0.5
@@ -25,7 +26,7 @@
 def kernel(trial, ham, partner_in, live_in, filt, gram,
            partner, live, hbuf, v0a, v0, v1, land0, land1, recv, gacc,
            core_out, core_in, tiles_out, tiles_in, own,
-           m_sem, h_sem, t_sem, halo_s, halo_r, y_s, y_r, c_s, c_r, p_s, p_r):
+           m_sem, h_sem, t_sem, halo_s, halo_r, y_s, y_r, c_s, c_r, p_s, p_r, relay):
     row = lax.axis_index("rows")
     col = lax.axis_index("cols")
     core = lax.rem(row, 2)
@@ -38,14 +39,13 @@
     def at_y(d):
         return (row, lax.rem(col + d, 4))
 
-    def at_plane(dz, dx):
-        return (lax.rem(pz + dz, 4) * 8 + lax.rem(px + dx, 4) * 2 + core, col)
-
-    peers = [after, before, mate] + [at_y(d) for d in (1, 2, 3)]
-    peers += [at_plane(n // 4, n % 4) for n in range(1, 16)]
-    barrier = pltpu.get_barrier_semaphore()
-    for peer in peers:
-        pl.semaphore_signal(barrier, inc=1, device_id=peer, device_id_type=MESH)
+    def at_x(d):
+        return (pz * 8 + lax.rem(px + d, 4) * 2 + core, col)
+
+    def at_z(d):
+        return (lax.rem(pz + d, 4) * 8 + px * 2 + core, col)
+
+    peers = [after, before, mate] + [f(d) for f in (at_y, at_x, at_z) for d in (1, 2, 3)]
 
     def remote(src, dst, ssem, rsem, peer):
         return pltpu.make_async_remote_copy(
@@ -57,7 +57,7 @@
         return pltpu.make_async_copy(ham.at[part], hbuf.at[part], h_sem.at[b])
 
     def block_of(i):
-        return jnp.where(i < 7, i + 1, jnp.where(i < 9, (8 - i) * (NG - 1), i - 1))
+        return jnp.where(i < MID, i + 1, jnp.where(i < MID + 2, (MID + 1 - i) * (NG - 1), i - 1))
 
     def start_ham(i, c):
         load_ham(block_of(i)).start()
@@ -67,11 +67,15 @@
     live = live_in
     load_head = pltpu.make_async_copy(trial.at[pl.ds(0, HEAD)], v0a.at[pl.ds(HW, HEAD)], t_sem.at[0])
     load_trial = pltpu.make_async_copy(trial, v0.at[pl.ds(HW, S)], t_sem.at[1])
+    load_head.start()
+    load_ham(block_of(0)).start()
     load_partner.start()
-    load_head.start()
-    for i in range(3):
+    for i in (1, 2):
         load_ham(block_of(i)).start()
     load_trial.start()
+    barrier = pltpu.get_barrier_semaphore()
+    for peer in peers:
+        pl.semaphore_signal(barrier, inc=1, device_id=peer, device_id_type=MESH)
     lax.fori_loop(3, NG, start_ham, 0)
     count = live[0]
 
@@ -79,7 +83,7 @@
         return (s < HW) | (s >= HW + S - count)
 
     def mask(ref, s):
-        ref[s + HW] = jnp.where(keep(s), ref[s + HW].astype(F32), 0.0).astype(BF)
+        ref[s + HW] = jnp.where(keep(s), ref[s + HW], jnp.zeros((B, B), BF))
 
     def product(src, s):
         lhs = jnp.concatenate([hbuf[s, k] for k in range(K)], axis=1)
@@ -92,11 +96,11 @@
             value = (product(src, s) - CENTER * src[s + HW].astype(F32)) * (1.0 / HALF_WIDTH)
             v1[s + HW] = jnp.where(keep(s), value, 0.0).astype(BF)
 
-    def second_step(g):
+    def second_step(g, src):
         for j in range(GS):
             s = g * GS + j
             value = (product(v1, s) - CENTER * v1[s + HW].astype(F32)) * (2.0 / HALF_WIDTH)
-            value = value - v0[s + HW].astype(F32)
+            value = value - src[s + HW].astype(F32)
             filt[s] = jnp.where(keep(s), value, 0.0).astype(BF)
 
     def to_col(g, t, d):
@@ -123,11 +127,12 @@
         return c
 
     lax.fori_loop(0, 3, prologue, 0)
-    load_trial.wait()
-    lax.fori_loop(HW, S - 32, lambda s, c: (mask(v0, s), c)[1], 0)
-    second_step(2)
+    second_step(2, v0a)
     pl.semaphore_wait(barrier, len(peers))
     hand_out(2, 0)
+
+    for d in (1, 2, 3):
+        pl.semaphore_signal(relay, inc=1, device_id=at_x(d), device_id_type=MESH)
 
     def halo(src, first, land, n):
         return (
@@ -143,16 +148,18 @@
     halo0 = halo(trial, 0, land0, 0)
     for copy in halo0:
         copy.start()
+    load_trial.wait()
+    lax.fori_loop(HW, S - 32, lambda s, c: (mask(v0, s), c)[1], 0)
 
     def main(i, c):
         b = i + 1
         load_ham(b).wait()
         first_step(b, v0)
-        second_step(i)
+        second_step(i, v0)
         hand_out(i, i - 2)
         return c
 
-    lax.fori_loop(3, 7, main, 0)
+    lax.fori_loop(3, MID, main, 0)
 
     for copy in halo0:
         copy.wait()
@@ -169,7 +176,9 @@
     for copy in halo1:
         copy.start()
 
-    lax.fori_loop(7, NG - 2, main, 0)
+    lax.fori_loop(MID, NG - 2, main, 0)
+
+    pl.semaphore_wait(relay, 3)
 
     def last(n, c):
         g = jnp.where(n == 0, NG - 2, jnp.where(n < 3, 2 - n, NG - 1))
@@ -180,7 +189,7 @@
                 copy.wait()
             place(land1, v1)
 
-        second_step(g)
+        second_step(g, v0)
         hand_out(g, NG - 4 + n)
         return c
 
@@ -303,6 +312,7 @@
             dma((4,)),
             dma((1,)),
             dma((1,)),
+            pltpu.SemaphoreType.REGULAR,
         ],
         compiler_params=pltpu.CompilerParams(
             collective_id=0, has_side_effects=True, vmem_limit_bytes=48 << 20),

time: 50 us -> 48.6 us (0.972)
  Pallas kernels: 48.6 us -> 47.2 us
    pallas_call x1, Pallas kernels: 47.2 us -> 45.8 us  [body(): pl.pallas_call(kernel, out_shape=shapes, in_specs=[hbm, hbm, hbm, pl.Bloc...]
where the time goes in v3:
time: 48.6 us; the launch traced here: 48.5 us
  Pallas kernels  47.2 us (97%)
  between operations  1.28 us (3%)
    pallas_call x1, Pallas kernels, body(): pl.pallas_call(kernel, out_shape=shapes, in_specs=[hbm, hbm, hbm, pl.Bloc...  45.8 us
    pallas_call x1, Pallas kernels, body(): pl.pallas_call(store, out_shape=shapes, in_specs=[vmem, vmem], out_specs=...  1.45 us

profile of v3, /device:TPU:1, one launch (start us, length us, event | category | flops | bytes accessed | tf_op | source)
XLA Modules:
  0.0 48.5 jit_solution(14706808602019687432)
XLA Ops:
  1.3 45.8 %filter_gram.1 = (bf16[72,128,128]{2,1,0:T(8,128)(2,1)S(1)}, f32[16,128]{1,0:T(8,128)S(1)}) custom-call(bf16[72,128,128]{2,1,0:T(8,128)(2,1)} %bitcast.3, bf16[72,9,128,128]{3,2,1,0:T(8,128)(2,1)} %ham.1, s32[9,72]{1,0:T(8,128)} %bitcast.4, s32[1]{0:T(128)S(6)} %copy.6.live_in), custom_call_target="tpu_custom_call" | custom-call | tf_op jit(solution)/shard_map/filter_gram/pallas_call | solution.py:283
  47.1 1.4 %store.1 = (bf16[72,128,128]{2,1,0:T(8,128)(2,1)}, f32[16,128]{1,0:T(8,128)}) custom-call(bf16[72,128,128]{2,1,0:T(8,128)(2,1)S(1)} %get-tuple-element.6.filt, f32[16,128]{1,0:T(8,128)S(1)} %get-tuple-element.7.gram), custom_call_target="tpu_custom_call" | custom-call | tf_op jit(solution)/shard_map/store/pallas_call | solution.py:321

commit v4 on v3

--- a/solution.py
+++ b/solution.py
@@ -265,10 +265,9 @@
 
 def store(filt, gram, filt_out, gram_out, sem):
     copies = [
-        pltpu.make_async_copy(filt.at[pl.ds(n * (S // 4), S // 4)], filt_out.at[pl.ds(n * (S // 4), S // 4)], sem.at[n])
-        for n in range(4)
+        pltpu.make_async_copy(gram, gram_out, sem.at[0]),
+        pltpu.make_async_copy(filt, filt_out, sem.at[1]),
     ]
-    copies.append(pltpu.make_async_copy(gram, gram_out, sem.at[4]))
     for copy in copies:
         copy.start()
     for copy in copies:
@@ -323,7 +322,7 @@
         out_shape=shapes,
         in_specs=[vmem, vmem],
         out_specs=(hbm, hbm),
-        scratch_shapes=[dma((5,))],
+        scratch_shapes=[dma((2,))],
         name="store",
     )(*[pltpu.with_memory_space_constraint(a, pltpu.VMEM) for a in (filtered, gram)])
     return filtered.reshape(S * B, B), gram

time: 48.6 us -> 48.6 us (level)
  no operation moved by 1% of the time
where the time goes in v4:
time: 48.6 us; the launch traced here: 48.5 us
  Pallas kernels  47.2 us (97%)
  between operations  1.28 us (3%)
    pallas_call x1, Pallas kernels, body(): pl.pallas_call(kernel, out_shape=shapes, in_specs=[hbm, hbm, hbm, pl.Bloc...  45.8 us
    pallas_call x1, Pallas kernels, body(): pl.pallas_call(store, out_shape=shapes, in_specs=[vmem, vmem], out_specs=...  1.43 us

profile of v4, /device:TPU:1, one launch (start us, length us, event | category | flops | bytes accessed | tf_op | source)
XLA Modules:
  0.0 48.5 jit_solution(191216953805274980)
XLA Ops:
  1.3 45.8 %filter_gram.1 = (bf16[72,128,128]{2,1,0:T(8,128)(2,1)S(1)}, f32[16,128]{1,0:T(8,128)S(1)}) custom-call(bf16[72,128,128]{2,1,0:T(8,128)(2,1)} %bitcast.3, bf16[72,9,128,128]{3,2,1,0:T(8,128)(2,1)} %ham.1, s32[9,72]{1,0:T(8,128)} %bitcast.4, s32[1]{0:T(128)S(6)} %copy.6.live_in), custom_call_target="tpu_custom_call" | custom-call | tf_op jit(solution)/shard_map/filter_gram/pallas_call | solution.py:282
  47.1 1.4 %store.1 = (bf16[72,128,128]{2,1,0:T(8,128)(2,1)}, f32[16,128]{1,0:T(8,128)}) custom-call(bf16[72,128,128]{2,1,0:T(8,128)(2,1)S(1)} %get-tuple-element.6.filt, f32[16,128]{1,0:T(8,128)S(1)} %get-tuple-element.7.gram), custom_call_target="tpu_custom_call" | custom-call | tf_op jit(solution)/shard_map/store/pallas_call | solution.py:320
